TPU v7x, 1024 devices: a whole 4x4x32 slice. The times are simulated.
1024 devices in a mesh: dp: 32 (over y, x, core), expert: 32 (over z).
Axes of the slice: x: 4, y: 4, z: 32, core: 2. Of those that a mesh axis runs over, the one named last changes fastest.
Arguments:
- token_values: bfloat16 [131072, 2560], P(('dp', 'expert')), may hold values from -6 to 6
- token_scales: float32 [131072, 20], P(('dp', 'expert')), may hold values from 0.25 to 4
- out_grad: bfloat16 [131072, 2560], P(('dp', 'expert')), may hold values from -6 to 6
- route_expert: int32 [131072, 1], P(('dp', 'expert')), may hold values from 0 to 31; in each aligned block of 128 rows (0 to 127, 128 to 255, ...) at most 5 rows name the same one
- gate: bfloat16 [131072, 1], P(('dp', 'expert')), may hold values from 0.049804688 to 1
- up_weight: bfloat16 [32, 2560, 768], P('expert'), may hold values from -0.125 to 0.125
- down_weight: bfloat16 [32, 768, 2560], P('expert'), may hold values from -0.21875 to 0.21875
Outputs:
- token_grad: bfloat16 [131072, 2560], P(('dp', 'expert'))
- gate_grad: bfloat16 [131072, 1], P(('dp', 'expert'))
- down_grad: float32 [32, 768, 2560], P('expert', 'dp')
Inputs may be any that keep to these rules, and one draw needn't show every extreme that they name: `route_expert`: among the rows of one device no expert is named by more than 5 routes; on some device one expert is named by exactly 5.
All inputs are finite; a program needn't handle non-finite values.
Results may differ from a plain program's by a relative error of at most 0.018.
Values may be sent and summed in bfloat16 or wider, within the bound.
A program may use at most 64 MiB of HBM per device.

v0:
```python
import jax
import jax.numpy as jnp
from jax import lax
from jax.sharding import PartitionSpec as P


def dequantize(values, scales):
    count, width = values.shape
    blocks = scales.shape[1]
    wide = values.astype(jnp.float32).reshape(count, blocks, width // blocks) * scales[:, :, None]
    return wide.reshape(count, width).astype(jnp.bfloat16)


def place_slots(route_ids, experts, capacity):
    flat = route_ids.reshape(-1)
    onehot = (flat[:, None] == jnp.arange(experts, dtype=jnp.int32)[None, :]).astype(jnp.int32)
    before = jnp.cumsum(onehot, axis=0) - onehot
    rank = jnp.sum(before * onehot, axis=1)
    return flat * capacity + rank


def expert_pass(inputs, grads, gates, up_w, down_w):
    pre = jnp.dot(inputs, up_w, preferred_element_type=jnp.float32)
    hidden = jax.nn.silu(pre).astype(jnp.bfloat16)
    back = lax.dot_general(
        grads, down_w, (((1,), (1,)), ((), ())), preferred_element_type=jnp.float32
    )
    gate_col = gates.astype(jnp.float32)[:, None]
    gate_term = jnp.sum(hidden.astype(jnp.float32) * back, axis=1).astype(jnp.bfloat16)
    sig = jax.nn.sigmoid(pre)
    pre_grad = (gate_col * back * sig * (1.0 + pre * (1.0 - sig))).astype(jnp.bfloat16)
    row_grad = lax.dot_general(
        pre_grad, up_w, (((1,), (1,)), ((), ())), preferred_element_type=jnp.float32
    ).astype(jnp.bfloat16)
    scaled = (gate_col * grads.astype(jnp.float32)).astype(jnp.bfloat16)
    return (row_grad, gate_term, hidden, scaled)


def body(token_values, token_scales, out_grad, route_expert, gate, up_weight, down_weight):
    experts = lax.axis_size("expert")
    tok_rows, width = token_values.shape
    routes = route_expert.shape[1]
    capacity = tok_rows * routes // experts + 1
    inputs = dequantize(token_values, token_scales)
    slots = place_slots(route_expert, experts, capacity)
    x_rows = jnp.repeat(inputs, routes, axis=0)
    g_rows = jnp.repeat(out_grad, routes, axis=0)
    x_buf = jnp.zeros((experts * capacity, width), jnp.bfloat16).at[slots].set(x_rows)
    g_buf = jnp.zeros((experts * capacity, width), jnp.bfloat16).at[slots].set(g_rows)
    w_buf = jnp.zeros((experts * capacity, 1), jnp.bfloat16).at[slots].set(gate)
    arrived = (
        lax.all_to_all(
            x_buf.reshape(experts, capacity, width),
            "expert",
            split_axis=0,
            concat_axis=0,
            tiled=True,
        ),
        lax.all_to_all(
            g_buf.reshape(experts, capacity, width),
            "expert",
            split_axis=0,
            concat_axis=0,
            tiled=True,
        ),
        lax.all_to_all(
            w_buf.reshape(experts, capacity, 1), "expert", split_axis=0, concat_axis=0, tiled=True
        ),
    )
    x_in = arrived[0].reshape(experts * capacity, width)
    g_in = arrived[1].reshape(experts * capacity, width)
    w_in = arrived[2].reshape(experts * capacity)
    row_grad, gate_term, hidden, scaled = expert_pass(
        x_in, g_in, w_in, up_weight[0], down_weight[0]
    )
    returned = (
        lax.all_to_all(
            row_grad.reshape(experts, capacity, width),
            "expert",
            split_axis=0,
            concat_axis=0,
            tiled=True,
        ),
        lax.all_to_all(
            gate_term.reshape(experts, capacity, 1),
            "expert",
            split_axis=0,
            concat_axis=0,
            tiled=True,
        ),
    )
    rows_back = returned[0].reshape(experts * capacity, width)[slots]
    token_grad = jnp.sum(
        rows_back.reshape(tok_rows, routes, width).astype(jnp.float32), axis=1
    ).astype(jnp.bfloat16)
    gate_grad = returned[1].reshape(experts * capacity)[slots].reshape(tok_rows, routes)
    partial_value = lax.dot_general(
        hidden, scaled, (((0,), (0,)), ((), ())), preferred_element_type=jnp.float32
    )
    summed = lax.psum_scatter(
        partial_value.astype(jnp.bfloat16), "dp", scatter_dimension=0, tiled=True
    ).astype(jnp.float32)
    return (token_grad, gate_grad, summed[None])


def solution(mesh):
    return jax.shard_map(
        body,
        mesh=mesh,
        in_specs=(
            P(("dp", "expert"), None),
            P(("dp", "expert"), None),
            P(("dp", "expert"), None),
            P(("dp", "expert"), None),
            P(("dp", "expert"), None),
            P("expert", None, None),
            P("expert", None, None),
        ),
        out_specs=(P(("dp", "expert"), None), P(("dp", "expert"), None), P("expert", "dp", None)),
        check_vma=False,
    )
```

profile of v0, /device:TPU:1, one launch (start us, length us, event | category | flops | bytes accessed | tf_op | source)
XLA Modules:
  0.0 506.2 jit_solution(8172271993991743156)
XLA Ops:
  7.2 0.7 fusion.17
  7.9 0.2 reduce_window_sum.11
  8.1 0.8 select_reduce_fusion
  8.9 0.7 fusion.18
  9.6 1.5 scatter_custom_fusion
  11.1 0.7 reshape.117
  11.8 29.3 %all-to-all-start = ((bf16[32,5,1]{1,2,0:T(2,128)(2,1)}), bf16[32,5,1]{1,2,0:T(2,128)(2,1)S(1)}, u32[]{:S(2)}, u32[]{:S(2)}) async-start(bf16[32,5,1]{1,2,0:T(2,128)(2,1)} %reshape.117), calls=%async_computation | async-start | bytes 32768 | tf_op jit(solution)/shard_map/all_to_all | solution.py:66
  41.1 1.4 copy.14
  42.5 0.8 fusion.9
  43.3 0.3 copy.15
  43.6 1.8 scatter_custom_fusion.2
  45.4 1.2 reshape.66
  46.6 15.6 %all-to-all-done = bf16[32,5,1]{1,2,0:T(2,128)(2,1)S(1)} async-done(((bf16[32,5,1]{1,2,0:T(2,128)(2,1)}), bf16[32,5,1]{1,2,0:T(2,128)(2,1)S(1)}, u32[]{:S(2)}, u32[]{:S(2)}) %all-to-all-start) | async-done | bytes 352 | tf_op jit(solution)/shard_map/all_to_all | solution.py:66
  62.3 5.6 %all-to-all-start.2 = ((bf16[32,5,2560]{2,1,0:T(8,128)(2,1)}), bf16[32,5,2560]{2,1,0:T(8,128)(2,1)S(1)}, u32[]{:S(2)}, u32[]{:S(2)}) async-start(bf16[32,5,2560]{2,1,0:T(8,128)(2,1)} %reshape.66), calls=%async_computation.2 | async-start | bytes 2621440 | tf_op jit(solution)/shard_map/all_to_all | solution.py:52
  67.9 2.3 scatter_custom_fusion.1
  70.2 1.3 reshape.64
  71.4 121.2 %all-to-all-done.2 = bf16[32,5,2560]{2,1,0:T(8,128)(2,1)S(1)} async-done(((bf16[32,5,2560]{2,1,0:T(8,128)(2,1)}), bf16[32,5,2560]{2,1,0:T(8,128)(2,1)S(1)}, u32[]{:S(2)}, u32[]{:S(2)}) %all-to-all-start.2) | async-done | bytes 819232 | tf_op jit(solution)/shard_map/all_to_all | solution.py:52
  192.6 10.3 %all-to-all-start.1 = ((bf16[32,5,2560]{2,1,0:T(8,128)(2,1)}), bf16[32,5,2560]{2,1,0:T(8,128)(2,1)S(1)}, u32[]{:S(2)}, u32[]{:S(2)}) async-start(bf16[32,5,2560]{2,1,0:T(8,128)(2,1)} %reshape.64), calls=%async_computation.1 | async-start | bytes 2621440 | tf_op jit(solution)/shard_map/all_to_all | solution.py:59
  202.9 0.1 convert_reduce_fusion
  203.0 0.1 reshape.72
  203.1 0.4 reshape.67
  203.5 2.9 fusion.2
  206.4 121.3 %all-to-all-done.1 = bf16[32,5,2560]{2,1,0:T(8,128)(2,1)S(1)} async-done(((bf16[32,5,2560]{2,1,0:T(8,128)(2,1)}), bf16[32,5,2560]{2,1,0:T(8,128)(2,1)S(1)}, u32[]{:S(2)}, u32[]{:S(2)}) %all-to-all-start.1) | async-done | bytes 819232 | tf_op jit(solution)/shard_map/all_to_all | solution.py:59
  327.7 0.4 reshape.65
  328.1 3.6 multiply_reduce_fusion
  331.8 0.7 convert_element_type.74
  332.5 10.3 %all-to-all-start.4 = ((bf16[32,5,1]{1,2,0:T(2,128)(2,1)}), bf16[32,5,1]{1,2,0:T(2,128)(2,1)S(1)}, u32[]{:S(2)}, u32[]{:S(2)}) async-start(bf16[32,5,1]{1,2,0:T(2,128)(2,1)} %convert_element_type.74), calls=%async_computation.4 | async-start | bytes 32768 | tf_op jit(solution)/shard_map/all_to_all | solution.py:84
  342.8 0.0 reduce-scatter.2.cloned.1.call-start
  342.9 3.2 convolution_convert_fusion
  346.0 0.0 reduce-scatter.2.cloned.1.call-update
  346.1 3.6 fusion.6
  349.7 1.3 reshape.68
  351.0 13.0 %all-to-all-done.4 = bf16[32,5,1]{1,2,0:T(2,128)(2,1)S(1)} async-done(((bf16[32,5,1]{1,2,0:T(2,128)(2,1)}), bf16[32,5,1]{1,2,0:T(2,128)(2,1)S(1)}, u32[]{:S(2)}, u32[]{:S(2)}) %all-to-all-start.4) | async-done | bytes 352 | tf_op jit(solution)/shard_map/all_to_all | solution.py:84
  364.0 8.2 %all-to-all-start.3 = ((bf16[32,5,2560]{2,1,0:T(8,128)(2,1)}), bf16[32,5,2560]{2,1,0:T(8,128)(2,1)S(1)}, u32[]{:S(2)}, u32[]{:S(2)}) async-start(bf16[32,5,2560]{2,1,0:T(8,128)(2,1)} %reshape.68), calls=%async_computation.3 | async-start | bytes 2621440 | tf_op jit(solution)/shard_map/all_to_all | solution.py:77
  372.2 0.1 reduce.1
  372.3 0.1 reshape.70
  372.4 1.7 gather_fusion.1
  374.1 110.2 %reduce-scatter.2.cloned.1.call-done = bf16[24,2560]{1,0:T(8,128)(2,1)} async-done(((bf16[768,2560]{1,0:T(8,128)(2,1)}), bf16[24,2560]{1,0:T(8,128)(2,1)}) %reduce-scatter.2.cloned.1.call-update) | async-done | bytes 122896 | tf_op jit(solution)/shard_map/reduce_scatter | solution.py:100
  484.3 1.6 bitcast_convert_fusion
  485.9 11.2 %all-to-all-done.3 = bf16[32,5,2560]{2,1,0:T(8,128)(2,1)S(1)} async-done(((bf16[32,5,2560]{2,1,0:T(8,128)(2,1)}), bf16[32,5,2560]{2,1,0:T(8,128)(2,1)S(1)}, u32[]{:S(2)}, u32[]{:S(2)}) %all-to-all-start.3) | async-done | bytes 819232 | tf_op jit(solution)/shard_map/all_to_all | solution.py:77
  497.1 0.4 reshape.69
  497.5 1.8 gather_fusion
  (1 shorter events, 0.0 us)
Async XLA Ops:
  11.8 50.5 %all-to-all-start = ((bf16[32,5,1]{1,2,0:T(2,128)(2,1)}), bf16[32,5,1]{1,2,0:T(2,128)(2,1)S(1)}, u32[]{:S(2)}, u32[]{:S(2)}) async-start(bf16[32,5,1]{1,2,0:T(2,128)(2,1)} %reshape.117), calls=%async_computation | async-start | bytes 32768 | tf_op jit(solution)/shard_map/all_to_all | solution.py:66
  62.3 130.4 %all-to-all-start.2 = ((bf16[32,5,2560]{2,1,0:T(8,128)(2,1)}), bf16[32,5,2560]{2,1,0:T(8,128)(2,1)S(1)}, u32[]{:S(2)}, u32[]{:S(2)}) async-start(bf16[32,5,2560]{2,1,0:T(8,128)(2,1)} %reshape.66), calls=%async_computation.2 | async-start | bytes 2621440 | tf_op jit(solution)/shard_map/all_to_all | solution.py:52
  192.6 135.1 %all-to-all-start.1 = ((bf16[32,5,2560]{2,1,0:T(8,128)(2,1)}), bf16[32,5,2560]{2,1,0:T(8,128)(2,1)S(1)}, u32[]{:S(2)}, u32[]{:S(2)}) async-start(bf16[32,5,2560]{2,1,0:T(8,128)(2,1)} %reshape.64), calls=%async_computation.1 | async-start | bytes 2621440 | tf_op jit(solution)/shard_map/all_to_all | solution.py:59
  332.5 31.5 %all-to-all-start.4 = ((bf16[32,5,1]{1,2,0:T(2,128)(2,1)}), bf16[32,5,1]{1,2,0:T(2,128)(2,1)S(1)}, u32[]{:S(2)}, u32[]{:S(2)}) async-start(bf16[32,5,1]{1,2,0:T(2,128)(2,1)} %convert_element_type.74), calls=%async_computation.4 | async-start | bytes 32768 | tf_op jit(solution)/shard_map/all_to_all | solution.py:84
  342.8 141.5 %reduce-scatter.2.cloned.1.call-start = ((), (), s32[]{:S(2)}) async-start(), calls=%async_computation.6 | async-start | bytes 4055040 | tf_op jit(solution)/shard_map/reduce_scatter | solution.py:100
  364.0 133.1 %all-to-all-start.3 = ((bf16[32,5,2560]{2,1,0:T(8,128)(2,1)}), bf16[32,5,2560]{2,1,0:T(8,128)(2,1)S(1)}, u32[]{:S(2)}, u32[]{:S(2)}) async-start(bf16[32,5,2560]{2,1,0:T(8,128)(2,1)} %reshape.68), calls=%async_computation.3 | async-start | bytes 2621440 | tf_op jit(solution)/shard_map/all_to_all | solution.py:77
Sparse Core Ops, SparseCore 0:
  349.4 134.9 reduce-scatter.1
where the time goes:
time: 508 us; the launch traced here: 506 us
  waiting for transfers between devices  393 us (77%)
  starting transfers between devices  63.7 us (13%)
  local copies, waits for them, and re-layouts  17.3 us (3%)
  between operations  14.2 us (3%)
  matrix products  13.4 us (3%)
    all_to_all x1, waiting for transfers between devices, body(): lax.all_to_all(g_buf.reshape(experts, capacity, width), 'expert', split_a...  121 us
    all_to_all x1, waiting for transfers between devices, body(): lax.all_to_all(x_buf.reshape(experts, capacity, width), 'expert', split_a...  121 us
    reduce_scatter x1, waiting for transfers between devices, body(): lax.psum_scatter(partial_value.astype(jnp.bfloat16), 'dp', scatter_dimens...  110 us
    all_to_all x1, starting transfers between devices, body(): lax.all_to_all(w_buf.reshape(experts, capacity, 1), 'expert', split_axis=...  29.3 us
    all_to_all x1, waiting for transfers between devices, body(): lax.all_to_all(w_buf.reshape(experts, capacity, 1), 'expert', split_axis=...  15.6 us
    all_to_all x1, waiting for transfers between devices, body(): lax.all_to_all(gate_term.reshape(experts, capacity, 1), 'expert', split_a...  13 us
    all_to_all x1, waiting for transfers between devices, body(): lax.all_to_all(row_grad.reshape(experts, capacity, width), 'expert', spli...  11.2 us
    all_to_all x1, starting transfers between devices, body(): lax.all_to_all(gate_term.reshape(experts, capacity, 1), 'expert', split_a...  10.3 us
  transfers between devices with their start and end apart: 6, of which 6 were waited for; matrix products, arithmetic and copies ran while one was open for 5% of the time, Pallas kernels for 0%

commit v1 on v0

v1 whole, which is shorter than its diff:
```python
import jax
import jax.numpy as jnp
from jax import lax
from jax.experimental import pallas as pl
from jax.experimental.pallas import tpu as pltpu
from jax.sharding import PartitionSpec as P

MESH = pl.DeviceIdType.MESH
BF = jnp.bfloat16
F32 = jnp.float32
I32 = jnp.int32

N = 32
TOK = 128
D = 2560
H = 768
CAP = 5
LANE = 128
CHUNKS = D // LANE
TILE = 16
FWD_TILES = 13
RET_TILES = 7
FIRST = (0, 3, 6, 9, 12)
SUB = 8
BATCHES = N // SUB
RB = 64
HALF = D // 2
OUT_ROWS = H // N


def offset_of(k):
    half = (k + 1) // 2
    return jnp.where(k % 2 == 1, 16 - half, 16 + half)


def first_group(tile):
    return 16 * (tile // 5) + FIRST[tile % 5]


def tile_key(owner, rank, tau, g):
    place = rank + (CAP * (FIRST[tau] + g) - TILE * tau)
    good = (place >= 0) & (place < TILE)
    return jnp.where(good, owner * TILE + place, -1)


def ones_where(mask):
    return jnp.where(mask, 1.0, 0.0).astype(BF)


def kernel(
    values_ref, scales_ref, grad_ref, route_ref, gate_ref, up_hbm, down_hbm,
    token_ref, gate_out_ref, down_ref,
    up_ref, dn_ref, stack, send, recv, ret, back, part, part_in, pack_m, pick_m, unpack_m, repack_m,
    xs, hid, sc,
    w_sem, fs_sem, fr_sem, bs_sem, br_sem, ps_sem, pr_sem,
):
    dp = lax.axis_index("dp")
    ex = lax.axis_index("expert")

    up_copy = pltpu.make_async_copy(up_hbm.at[0], up_ref, w_sem.at[0])
    down_copy = pltpu.make_async_copy(down_hbm.at[0], dn_ref, w_sem.at[1])
    up_copy.start()
    down_copy.start()

    barrier = pltpu.get_barrier_semaphore()

    @pl.loop(1, N)
    def _(s):
        pl.semaphore_signal(
            barrier, inc=1, device_id=(dp, lax.rem(ex + s, N)), device_id_type=MESH
        )
        pl.semaphore_signal(
            barrier, inc=1, device_id=(lax.rem(dp + s, N), ex), device_id_type=MESH
        )

    r_col = route_ref[...].astype(F32)
    wide = jnp.broadcast_to(r_col, (TOK, TOK))
    tall = wide.T
    rows_i = lax.broadcasted_iota(I32, (TOK, TOK), 0)
    cols_i = lax.broadcasted_iota(I32, (TOK, TOK), 1)
    same = wide == tall
    rank_row = jnp.sum(jnp.where(same & (rows_i < cols_i), 1.0, 0.0), axis=0, keepdims=True).astype(I32)
    rank_col = jnp.sum(jnp.where(same & (cols_i < rows_i), 1.0, 0.0), axis=1, keepdims=True).astype(I32)
    r_row = tall[0:1, :].astype(I32)
    r_col = route_ref[...]

    gate = gate_ref[...].astype(F32)
    for c in range(CHUNKS):
        cols = slice(c * LANE, (c + 1) * LANE)
        stack[c * TOK : (c + 1) * TOK, :] = (
            values_ref[:, cols].astype(F32) * scales_ref[:, c : c + 1]
        ).astype(BF)
        stack[(CHUNKS + c) * TOK : (CHUNKS + c + 1) * TOK, :] = (
            gate * grad_ref[:, cols].astype(F32)
        ).astype(BF)
    stack[2 * CHUNKS * TOK :, :] = jnp.zeros((2 * TOK, LANE), BF)

    big = N * TILE
    row_id = lax.broadcasted_iota(I32, (big, TOK), 0)
    lane_id = lax.broadcasted_iota(I32, (TOK, big), 1)
    for tau in range(5):
        for g in range(4):
            key = tile_key(r_row, rank_row, tau, g)
            pack_m[tau, :, g * TOK : (g + 1) * TOK] = ones_where(row_id == key)
    for t in range(FWD_TILES):
        first = first_group(t)
        got = jnp.dot(
            pack_m[t % 5], stack[first * TOK : (first + 4) * TOK, :], preferred_element_type=F32
        )
        send[:, t * TILE : (t + 1) * TILE, :] = got.astype(BF).reshape(N, TILE, LANE)

    pl.semaphore_wait(barrier, 2 * (N - 1))

    def forward(k):
        to = lax.rem(ex + offset_of(k), N)
        return pltpu.make_async_remote_copy(
            src_ref=send.at[to],
            dst_ref=recv.at[k],
            send_sem=fs_sem.at[k],
            recv_sem=fr_sem.at[k],
            device_id=(dp, to),
            device_id_type=MESH,
        )

    def backward(k):
        to = lax.rem(ex - offset_of(k) + N, N)
        return pltpu.make_async_remote_copy(
            src_ref=ret.at[k],
            dst_ref=back.at[ex],
            send_sem=bs_sem.at[k],
            recv_sem=br_sem.at[k],
            device_id=(dp, to),
            device_id_type=MESH,
        )

    def partial(s):
        to = lax.rem(dp + s, N)
        return pltpu.make_async_remote_copy(
            src_ref=part.at[to],
            dst_ref=part_in.at[s - 1],
            send_sem=ps_sem.at[s - 1],
            recv_sem=pr_sem.at[s - 1],
            device_id=(to, ex),
            device_id_type=MESH,
        )

    @pl.loop(0, N - 1)
    def _(k):
        forward(k).start()

    recv[N - 1] = send[ex]

    for tau in range(5):
        for g in range(4):
            key = tile_key(r_col, rank_col, tau, g)
            pick_m[tau, g * TOK : (g + 1) * TOK, :] = ones_where(lane_id == key)
    small = SUB * TILE
    w_row = lax.broadcasted_iota(I32, (RB, small), 0)
    w_lane = lax.broadcasted_iota(I32, (small, RB), 1)
    c_lane = lax.broadcasted_iota(I32, (RB, small), 1)
    c_row = lax.broadcasted_iota(I32, (small, RB), 0)
    for tau in range(5):
        for g in range(4):
            owner = (w_row * 52) >> 8
            key = tile_key(owner, w_row - CAP * owner, tau, g)
            unpack_m[tau, g * RB : (g + 1) * RB, :] = ones_where(
                (c_lane == key) & (w_row < SUB * CAP)
            )
            owner = (w_lane * 52) >> 8
            key = tile_key(owner, w_lane - CAP * owner, tau, g)
            repack_m[tau, :, g * RB : (g + 1) * RB] = ones_where(
                (c_row == key) & (w_lane < SUB * CAP)
            )
    up_copy.wait()
    down_copy.wait()

    lane_small = lax.broadcasted_iota(I32, (RB, LANE), 1)

    @pl.loop(0, BATCHES)
    def _(b):
        for i in range(SUB):
            k = b * SUB + i

            @pl.when(k < N - 1)
            def _():
                forward(k).wait_recv()

        @pl.when(b == BATCHES - 1)
        def _():
            @pl.loop(0, (BATCHES - 1) * SUB)
            def _(k):
                backward(k).start()

        here = pl.ds(pl.multiple_of(b * SUB, SUB), SUB)
        rows = pl.ds(pl.multiple_of(b * RB, RB), RB)
        carry = None
        for t in range(FWD_TILES):
            tile = recv[here, t * TILE : (t + 1) * TILE, :].reshape(small, LANE)
            got = jnp.dot(unpack_m[t % 5], tile, preferred_element_type=F32)
            for g in range(4):
                group = first_group(t) + g
                piece = got[g * RB : (g + 1) * RB]
                if g == 0 and t % 5 > 0:
                    piece = piece + carry
                if g == 3 and t % 5 < 4 and t < FWD_TILES - 1:
                    carry = piece
                    continue
                if group < CHUNKS:
                    xs[:, group * LANE : (group + 1) * LANE] = piece.astype(BF)
                elif group < 2 * CHUNKS:
                    at = (group - CHUNKS) * LANE
                    sc[rows, at : at + LANE] = piece.astype(BF)
        pre = jnp.dot(xs[...], up_ref[...], preferred_element_type=F32)
        back_g = lax.dot_general(
            sc[rows, :], dn_ref[...], (((1,), (1,)), ((), ())), preferred_element_type=F32
        )
        sig = 1.0 / (1.0 + jnp.exp(-pre))
        hidden = (pre * sig).astype(BF).astype(F32)
        hid[rows, :] = hidden
        term = jnp.sum(hidden * back_g, axis=1, keepdims=True)
        high = term.astype(BF).astype(F32)
        term_tile = jnp.where(lane_small < LANE // 2, high, term - high).astype(BF)
        pre_grad = (back_g * sig * (1.0 + pre * (1.0 - sig))).astype(BF)
        row_grad = lax.dot_general(
            pre_grad, up_ref[...], (((1,), (1,)), ((), ())), preferred_element_type=F32
        ).astype(BF)
        xs[...] = row_grad
        blank = jnp.zeros((RB, LANE), BF)
        for t in range(RET_TILES):
            pieces = []
            for g in range(4):
                group = first_group(t) + g
                if group < CHUNKS:
                    pieces.append(xs[:, group * LANE : (group + 1) * LANE])
                elif group == CHUNKS:
                    pieces.append(term_tile)
                else:
                    pieces.append(blank)
            got = jnp.dot(
                repack_m[t % 5], jnp.concatenate(pieces, axis=0), preferred_element_type=F32
            )
            ret[here, t * TILE : (t + 1) * TILE, :] = got.astype(BF).reshape(SUB, TILE, LANE)

    @pl.loop((BATCHES - 1) * SUB, N - 1)
    def _(k):
        backward(k).start()

    back[ex] = ret[N - 1]

    hid_t = hid[...].T.astype(BF)
    step = 256
    for n in range(HALF // step):
        left = jnp.dot(hid_t, sc[:, n * step : (n + 1) * step], preferred_element_type=F32)
        right = jnp.dot(
            hid_t, sc[:, HALF + n * step : HALF + (n + 1) * step], preferred_element_type=F32
        )
        both = jnp.concatenate(
            [left.reshape(N, OUT_ROWS, step), right.reshape(N, OUT_ROWS, step)], axis=1
        )
        part[:, :, n * step : (n + 1) * step] = both.astype(BF)

    @pl.loop(1, N)
    def _(s):
        partial(s).start()

    @pl.loop(0, N - 1)
    def _(k):
        backward(k).wait_recv()

    carry = None
    for t in range(RET_TILES):
        tile = back[:, t * TILE : (t + 1) * TILE, :].reshape(big, LANE)
        got = jnp.dot(pick_m[t % 5], tile, preferred_element_type=F32)
        for g in range(4):
            group = first_group(t) + g
            piece = got[g * TOK : (g + 1) * TOK]
            if g == 0 and t % 5 > 0:
                piece = piece + carry
            if g == 3 and t % 5 < 4 and t < RET_TILES - 1:
                carry = piece
                continue
            if group < CHUNKS:
                token_ref[:, group * LANE : (group + 1) * LANE] = piece.astype(BF)
            elif group == CHUNKS:
                total = piece[:, 0:1] + piece[:, LANE // 2 : LANE // 2 + 1]
                gate_out_ref[...] = (total / gate).astype(BF)

    @pl.loop(1, N)
    def _(s):
        partial(s).wait_recv()

    for n in range(HALF // step):
        cols = slice(n * step, (n + 1) * step)
        total = lax.fori_loop(
            0,
            N - 1,
            lambda s, acc: acc + part_in[s, :, cols].astype(F32),
            part[dp, :, cols].astype(F32),
        )
        down_ref[:, n * step : (n + 1) * step] = total[:OUT_ROWS]
        down_ref[:, HALF + n * step : HALF + (n + 1) * step] = total[OUT_ROWS:]

    @pl.loop(0, N - 1)
    def _(k):
        forward(k).wait_send()
        backward(k).wait_send()

    @pl.loop(1, N)
    def _(s):
        partial(s).wait_send()


def body(token_values, token_scales, out_grad, route_expert, gate, up_weight, down_weight):
    vmem = pl.BlockSpec(memory_space=pltpu.VMEM)
    hbm = pl.BlockSpec(memory_space=pl.ANY)
    dma = pltpu.SemaphoreType.DMA
    token_grad, gate_grad, down_grad = pl.pallas_call(
        kernel,
        out_shape=(
            jax.ShapeDtypeStruct((TOK, D), BF),
            jax.ShapeDtypeStruct((TOK, 1), BF),
            jax.ShapeDtypeStruct((OUT_ROWS, D), F32),
        ),
        in_specs=[vmem] * 5 + [hbm] * 2,
        out_specs=(vmem, vmem, vmem),
        scratch_shapes=[
            pltpu.VMEM((D, H), BF),
            pltpu.VMEM((H, D), BF),
            pltpu.VMEM(((2 * CHUNKS + 2) * TOK, LANE), BF),
            pltpu.VMEM((N, FWD_TILES * TILE, LANE), BF),
            pltpu.VMEM((N, FWD_TILES * TILE, LANE), BF),
            pltpu.VMEM((N, RET_TILES * TILE, LANE), BF),
            pltpu.VMEM((N, RET_TILES * TILE, LANE), BF),
            pltpu.VMEM((N, 2 * OUT_ROWS, HALF), BF),
            pltpu.VMEM((N - 1, 2 * OUT_ROWS, HALF), BF),
            pltpu.VMEM((5, N * TILE, 4 * TOK), BF),
            pltpu.VMEM((5, 4 * TOK, N * TILE), BF),
            pltpu.VMEM((5, 4 * RB, SUB * TILE), BF),
            pltpu.VMEM((5, SUB * TILE, 4 * RB), BF),
            pltpu.VMEM((RB, D), BF),
            pltpu.VMEM((BATCHES * RB, H), F32),
            pltpu.VMEM((BATCHES * RB, D), BF),
            dma((2,)),
            dma((N - 1,)),
            dma((N - 1,)),
            dma((N - 1,)),
            dma((N - 1,)),
            dma((N - 1,)),
            dma((N - 1,)),
        ],
        compiler_params=pltpu.CompilerParams(
            collective_id=0, has_side_effects=True, vmem_limit_bytes=52 * 2**20
        ),
    )(token_values, token_scales, out_grad, route_expert, gate, up_weight, down_weight)
    return token_grad, gate_grad, down_grad[None]


def solution(mesh):
    return jax.shard_map(
        body,
        mesh=mesh,
        in_specs=(
            P(("dp", "expert"), None),
            P(("dp", "expert"), None),
            P(("dp", "expert"), None),
            P(("dp", "expert"), None),
            P(("dp", "expert"), None),
            P("expert", None, None),
            P("expert", None, None),
        ),
        out_specs=(P(("dp", "expert"), None), P(("dp", "expert"), None), P("expert", "dp", None)),
        check_vma=False,
    )
```

time: 508 us -> 270 us (0.53)
  waiting for transfers between devices: 393 us -> 0 us
  Pallas kernels: 0 us -> 263 us
  starting transfers between devices: 63.7 us -> 0 us
  between operations: 14.2 us -> 0.65 us
  matrix products: 13.4 us -> 0 us
  local copies, waits for them, and re-layouts: 17.3 us -> 5.57 us
    all_to_all x5 -> x0, waiting for transfers between devices: 282 us -> none  [the longest x1 121 us: body(): lax.all_to_all(g_buf.reshape(experts, capacity, width), 'expert', split_a...]
    pallas_call x0 -> x1, Pallas kernels: none -> 263 us  [body(): pl.pallas_call(kernel, out_shape=(jax.ShapeDtypeStruct((TOK, D), BF), jax...]
    reduce_scatter x1 -> x0, waiting for transfers between devices: 110 us -> none  [body(): lax.psum_scatter(partial_value.astype(jnp.bfloat16), 'dp', scatter_dimens...]
    all_to_all x5 -> x0, starting transfers between devices: 63.6 us -> none  [the longest x1 29.3 us: body(): lax.all_to_all(w_buf.reshape(experts, capacity, 1), 'expert', split_axis=...]
    dot_general x4 -> x0, matrix products: 13.4 us -> none  [the longest x1 3.65 us: expert_pass(): lax.dot_general(pre_grad, up_w, (((1,), (1,)), ((), ())), preferred_eleme...]
    reshape x8 -> x0, local copies, waits for them, and re-layouts: 5.74 us -> none  [the longest x1 1.27 us: body(): row_grad.reshape(experts, capacity, width)]
    scatter x3 -> x0, local copies, waits for them, and re-layouts: 5.55 us -> none  [the longest x1 2.32 us: body(): jnp.zeros((experts * capacity, width), jnp.bfloat16).at[slots].set(g_rows)]
  transfers between devices with their start and end apart: 6 -> 0, of which waited for: 6 -> 0; matrix products, arithmetic and copies ran while one was open for 5% -> 0% of each run, Pallas kernels for 0% -> 0%
where the time goes in v1:
time: 270 us
  Pallas kernels  263 us (97%)
  local copies, waits for them, and re-layouts  5.57 us (2%)
    pallas_call x1, Pallas kernels, body(): pl.pallas_call(kernel, out_shape=(jax.ShapeDtypeStruct((TOK, D), BF), jax...  263 us
    unnamed x8, local copies, waits for them, and re-layouts  5.57 us

profile of v1, /device:TPU:1, one launch (start us, length us, event | category | flops | bytes accessed | tf_op | source)
XLA Modules:
  0.0 269.7 jit_solution(10009730965974301217)
XLA Ops:
  0.6 0.8 copy.12.gate_ref
  1.4 0.8 copy.10.scales_ref
  2.2 0.8 copy.11.route_ref
  3.0 0.0 copy-start
  3.0 1.1 copy-done
  4.1 263.5 %shard_map.94 = (bf16[128,2560]{1,0:T(8,128)(2,1)S(1)}, bf16[128,1]{1,0:T(8,128)(2,1)S(1)}, f32[24,2560]{1,0:T(8,128)S(1)}) custom-call(bf16[128,2560]{1,0:T(8,128)(2,1)S(1)} %copy-done, f32[128,20]{1,0:T(8,128)S(1)} %copy.10.scales_ref, bf16[128,2560]{1,0:T(8,128)(2,1)} %grad_ref.1, s32[128,1]{1,0:T(8,128)S(1)} %copy.11.route_ref, ...), custom_call_target="tpu_custom_call" | custom-call | tf_op jit(solution)/shard_map/pallas_call | solution.py:317
  267.6 0.6 copy.13
  268.2 0.8 copy.16
  269.0 0.7 copy.17
Async XLA Ops:
  3.0 1.1 copy-start

commit v2 on v1

--- a/solution.py
+++ b/solution.py
@@ -26,6 +26,9 @@
 RB = 64
 HALF = D // 2
 OUT_ROWS = H // N
+CHIPS = 16
+MSG = 2 * OUT_ROWS
+RELEASE = 2
 
 
 def offset_of(k):
@@ -50,12 +53,14 @@
 def kernel(
     values_ref, scales_ref, grad_ref, route_ref, gate_ref, up_hbm, down_hbm,
     token_ref, gate_out_ref, down_ref,
-    up_ref, dn_ref, stack, send, recv, ret, back, part, part_in, pack_m, pick_m, unpack_m, repack_m,
-    xs, hid, sc,
-    w_sem, fs_sem, fr_sem, bs_sem, br_sem, ps_sem, pr_sem,
+    up_ref, dn_ref, stack, send, recv, ret, back, part, pair_in, pair_sum, part_in, pack_m, pick_m, unpack_m, repack_m,
+    xs, hid, sc, square,
+    w_sem, fs_sem, fr_sem, bs_sem, br_sem, ps_sem, pr_sem, pair_s, pair_r,
 ):
     dp = lax.axis_index("dp")
     ex = lax.axis_index("expert")
+    chip = dp // 2
+    core = dp % 2
 
     up_copy = pltpu.make_async_copy(up_hbm.at[0], up_ref, w_sem.at[0])
     down_copy = pltpu.make_async_copy(down_hbm.at[0], dn_ref, w_sem.at[1])
@@ -73,48 +78,35 @@
             barrier, inc=1, device_id=(lax.rem(dp + s, N), ex), device_id_type=MESH
         )
 
-    r_col = route_ref[...].astype(F32)
-    wide = jnp.broadcast_to(r_col, (TOK, TOK))
-    tall = wide.T
+    tall = jnp.broadcast_to(route_ref[...].astype(F32), (TOK, TOK))
+    wide = tall.T
     rows_i = lax.broadcasted_iota(I32, (TOK, TOK), 0)
     cols_i = lax.broadcasted_iota(I32, (TOK, TOK), 1)
     same = wide == tall
     rank_row = jnp.sum(jnp.where(same & (rows_i < cols_i), 1.0, 0.0), axis=0, keepdims=True).astype(I32)
     rank_col = jnp.sum(jnp.where(same & (cols_i < rows_i), 1.0, 0.0), axis=1, keepdims=True).astype(I32)
-    r_row = tall[0:1, :].astype(I32)
-    r_col = route_ref[...]
-
-    gate = gate_ref[...].astype(F32)
+    r_row = route_ref[...]
+    r_col = wide[:, 0:1].astype(I32)
+    d_row = lax.rem(r_row - ex + N, N)
+
+    gate = jnp.broadcast_to(gate_ref[...].astype(F32), (TOK, TOK)).T[:, 0:1]
+    square[...] = jnp.zeros_like(square)
+    square[0:CHUNKS, :] = scales_ref[...]
+    scales = square[...].T
     for c in range(CHUNKS):
         cols = slice(c * LANE, (c + 1) * LANE)
         stack[c * TOK : (c + 1) * TOK, :] = (
-            values_ref[:, cols].astype(F32) * scales_ref[:, c : c + 1]
+            values_ref[:, cols].astype(F32) * scales[:, c : c + 1]
         ).astype(BF)
         stack[(CHUNKS + c) * TOK : (CHUNKS + c + 1) * TOK, :] = (
             gate * grad_ref[:, cols].astype(F32)
         ).astype(BF)
     stack[2 * CHUNKS * TOK :, :] = jnp.zeros((2 * TOK, LANE), BF)
 
-    big = N * TILE
-    row_id = lax.broadcasted_iota(I32, (big, TOK), 0)
-    lane_id = lax.broadcasted_iota(I32, (TOK, big), 1)
-    for tau in range(5):
-        for g in range(4):
-            key = tile_key(r_row, rank_row, tau, g)
-            pack_m[tau, :, g * TOK : (g + 1) * TOK] = ones_where(row_id == key)
-    for t in range(FWD_TILES):
-        first = first_group(t)
-        got = jnp.dot(
-            pack_m[t % 5], stack[first * TOK : (first + 4) * TOK, :], preferred_element_type=F32
-        )
-        send[:, t * TILE : (t + 1) * TILE, :] = got.astype(BF).reshape(N, TILE, LANE)
-
-    pl.semaphore_wait(barrier, 2 * (N - 1))
-
     def forward(k):
         to = lax.rem(ex + offset_of(k), N)
         return pltpu.make_async_remote_copy(
-            src_ref=send.at[to],
+            src_ref=send.at[offset_of(k)],
             dst_ref=recv.at[k],
             send_sem=fs_sem.at[k],
             recv_sem=fr_sem.at[k],
@@ -133,22 +125,61 @@
             device_id_type=MESH,
         )
 
+    pair_copy = pltpu.make_async_remote_copy(
+        src_ref=part.at[1 - core],
+        dst_ref=pair_in,
+        send_sem=pair_s.at[0],
+        recv_sem=pair_r.at[0],
+        device_id=(2 * chip + 1 - core, ex),
+        device_id_type=MESH,
+    )
+
     def partial(s):
-        to = lax.rem(dp + s, N)
+        to = lax.rem(chip + s, CHIPS)
         return pltpu.make_async_remote_copy(
-            src_ref=part.at[to],
+            src_ref=pair_sum.at[to],
             dst_ref=part_in.at[s - 1],
             send_sem=ps_sem.at[s - 1],
             recv_sem=pr_sem.at[s - 1],
-            device_id=(to, ex),
+            device_id=(2 * to + core, ex),
             device_id_type=MESH,
         )
 
-    @pl.loop(0, N - 1)
+    big = N * TILE
+    lane_id = lax.broadcasted_iota(I32, (TOK, big), 1)
+
+    def pack(low, high):
+        rows = slice(low * TILE, high * TILE)
+        count = high - low
+        row_id = lax.broadcasted_iota(I32, (count * TILE, TOK), 0) + low * TILE
+        for tau in range(5):
+            for g in range(4):
+                key = tile_key(d_row, rank_row, tau, g)
+                pack_m[tau, rows, g * TOK : (g + 1) * TOK] = ones_where(row_id == key)
+        for t in range(FWD_TILES):
+            first = first_group(t)
+            got = jnp.dot(
+                pack_m[t % 5, rows, :],
+                stack[first * TOK : (first + 4) * TOK, :],
+                preferred_element_type=F32,
+            )
+            send[low:high, t * TILE : (t + 1) * TILE, :] = got.astype(BF).reshape(count, TILE, LANE)
+
+    pack(8, 24)
+    pl.semaphore_wait(barrier, 2 * (N - 1))
+
+    @pl.loop(0, N // 2)
     def _(k):
         forward(k).start()
 
-    recv[N - 1] = send[ex]
+    pack(0, 8)
+    pack(24, N)
+
+    @pl.loop(N // 2, N - 1)
+    def _(k):
+        forward(k).start()
+
+    recv[N - 1] = send[0]
 
     for tau in range(5):
         for g in range(4):
@@ -185,9 +216,9 @@
             def _():
                 forward(k).wait_recv()
 
-        @pl.when(b == BATCHES - 1)
+        @pl.when(b == RELEASE)
         def _():
-            @pl.loop(0, (BATCHES - 1) * SUB)
+            @pl.loop(0, RELEASE * SUB)
             def _(k):
                 backward(k).start()
 
@@ -241,9 +272,13 @@
             )
             ret[here, t * TILE : (t + 1) * TILE, :] = got.astype(BF).reshape(SUB, TILE, LANE)
 
-    @pl.loop((BATCHES - 1) * SUB, N - 1)
-    def _(k):
-        backward(k).start()
+        @pl.when(b >= RELEASE)
+        def _():
+            @pl.loop(0, SUB)
+            def _(i):
+                @pl.when(b * SUB + i < N - 1)
+                def _():
+                    backward(b * SUB + i).start()
 
     back[ex] = ret[N - 1]
 
@@ -256,15 +291,51 @@
         )
         both = jnp.concatenate(
             [left.reshape(N, OUT_ROWS, step), right.reshape(N, OUT_ROWS, step)], axis=1
-        )
-        part[:, :, n * step : (n + 1) * step] = both.astype(BF)
-
-    @pl.loop(1, N)
+        ).astype(BF)
+        both = both.reshape(CHIPS, 2, MSG, step)
+        for c in range(2):
+            part[c, :, :, n * step : (n + 1) * step] = both[:, c]
+
+    pair_copy.start()
+    pair_copy.wait_recv()
+
+    @pl.loop(1, CHIPS + 1)
     def _(s):
-        partial(s).start()
+        to = lax.rem(chip + s, CHIPS)
+        pair_sum[to] = (part[core, to].astype(F32) + pair_in[to].astype(F32)).astype(BF)
+
+        @pl.when(s < CHIPS)
+        def _():
+            partial(s).start()
+
+    @pl.loop(1, CHIPS)
+    def _(s):
+        partial(s).wait_recv()
+
+    for n in range(HALF // step):
+        cols = slice(n * step, (n + 1) * step)
+        total = lax.fori_loop(
+            0,
+            CHIPS - 1,
+            lambda s, acc: acc + part_in[s, :, cols].astype(F32),
+            pair_sum[chip, :, cols].astype(F32),
+        )
+        down_ref[:, n * step : (n + 1) * step] = total[:OUT_ROWS]
+        down_ref[:, HALF + n * step : HALF + (n + 1) * step] = total[OUT_ROWS:]
 
     @pl.loop(0, N - 1)
     def _(k):
+        forward(k).wait_send()
+
+    @pl.loop(1, CHIPS)
+    def _(s):
+        partial(s).wait_send()
+
+    pair_copy.wait_send()
+
+    @pl.loop(0, N - 1)
+    def _(k):
+        backward(k).wait_send()
         backward(k).wait_recv()
 
     carry = None
@@ -284,30 +355,6 @@
             elif group == CHUNKS:
                 total = piece[:, 0:1] + piece[:, LANE // 2 : LANE // 2 + 1]
                 gate_out_ref[...] = (total / gate).astype(BF)
-
-    @pl.loop(1, N)
-    def _(s):
-        partial(s).wait_recv()
-
-    for n in range(HALF // step):
-        cols = slice(n * step, (n + 1) * step)
-        total = lax.fori_loop(
-            0,
-            N - 1,
-            lambda s, acc: acc + part_in[s, :, cols].astype(F32),
-            part[dp, :, cols].astype(F32),
-        )
-        down_ref[:, n * step : (n + 1) * step] = total[:OUT_ROWS]
-        down_ref[:, HALF + n * step : HALF + (n + 1) * step] = total[OUT_ROWS:]
-
-    @pl.loop(0, N - 1)
-    def _(k):
-        forward(k).wait_send()
-        backward(k).wait_send()
-
-    @pl.loop(1, N)
-    def _(s):
-        partial(s).wait_send()
 
 
 def body(token_values, token_scales, out_grad, route_expert, gate, up_weight, down_weight):
@@ -331,8 +378,10 @@
             pltpu.VMEM((N, FWD_TILES * TILE, LANE), BF),
             pltpu.VMEM((N, RET_TILES * TILE, LANE), BF),
             pltpu.VMEM((N, RET_TILES * TILE, LANE), BF),
-            pltpu.VMEM((N, 2 * OUT_ROWS, HALF), BF),
-            pltpu.VMEM((N - 1, 2 * OUT_ROWS, HALF), BF),
+            pltpu.VMEM((2, CHIPS, MSG, HALF), BF),
+            pltpu.VMEM((CHIPS, MSG, HALF), BF),
+            pltpu.VMEM((CHIPS, MSG, HALF), BF),
+            pltpu.VMEM((CHIPS - 1, MSG, HALF), BF),
             pltpu.VMEM((5, N * TILE, 4 * TOK), BF),
             pltpu.VMEM((5, 4 * TOK, N * TILE), BF),
             pltpu.VMEM((5, 4 * RB, SUB * TILE), BF),
@@ -340,18 +389,29 @@
             pltpu.VMEM((RB, D), BF),
             pltpu.VMEM((BATCHES * RB, H), F32),
             pltpu.VMEM((BATCHES * RB, D), BF),
+            pltpu.VMEM((TOK, TOK), F32),
             dma((2,)),
             dma((N - 1,)),
             dma((N - 1,)),
             dma((N - 1,)),
             dma((N - 1,)),
-            dma((N - 1,)),
-            dma((N - 1,)),
+            dma((CHIPS - 1,)),
+            dma((CHIPS - 1,)),
+            dma((1,)),
+            dma((1,)),
         ],
         compiler_params=pltpu.CompilerParams(
             collective_id=0, has_side_effects=True, vmem_limit_bytes=52 * 2**20
         ),
-    )(token_values, token_scales, out_grad, route_expert, gate, up_weight, down_weight)
+    )(
+        token_values,
+        token_scales.T,
+        out_grad,
+        route_expert.reshape(1, TOK),
+        gate.reshape(1, TOK),
+        up_weight,
+        down_weight,
+    )
     return token_grad, gate_grad, down_grad[None]
 
 

time: 270 us -> 265 us (0.981)
  Pallas kernels: 263 us -> 259 us
    pallas_call x1, Pallas kernels: 263 us -> 259 us  [body(): pl.pallas_call(kernel, out_shape=(jax.ShapeDtypeStruct((TOK, D), BF), jax...]
    unnamed x8 -> x11, local copies, waits for them, and re-layouts: 5.57 us -> 5.22 us
where the time goes in v2:
time: 265 us
  Pallas kernels  259 us (98%)
  local copies, waits for them, and re-layouts  5.22 us (2%)
    pallas_call x1, Pallas kernels, body(): pl.pallas_call(kernel, out_shape=(jax.ShapeDtypeStruct((TOK, D), BF), jax...  259 us

profile of v2, /device:TPU:1, one launch (start us, length us, event | category | flops | bytes accessed | tf_op | source)
XLA Modules:
  0.0 264.9 jit_solution(14911098973039745162)
XLA Ops:
  0.6 0.0 copy-start
  0.6 1.1 copy-done
  1.7 0.0 copy-start.1
  1.7 0.7 copy-done.1
  2.4 0.0 copy-start.2
  2.4 0.7 copy-done.2
  3.1 0.0 copy-start.3
  3.1 0.7 copy-done.3
  3.7 259.0 %shard_map.94 = (bf16[128,2560]{1,0:T(8,128)(2,1)S(1)}, bf16[128,1]{1,0:T(8,128)(2,1)S(1)}, f32[24,2560]{1,0:T(8,128)S(1)}) custom-call(bf16[128,2560]{1,0:T(8,128)(2,1)S(1)} %copy-done, f32[20,128]{1,0:T(8,128)S(1)} %bitcast.5, bf16[128,2560]{1,0:T(8,128)(2,1)} %grad_ref.1, s32[1,128]{1,0:T(1,128)S(1)} %bitcast.6, bf16[1,128]{1,0:T(2,128)(2,1)S(1)} %bitcast.7, ...), custom_call_target="tpu_custom_call" | custom-call | tf_op jit(solution)/shard_map/pallas_call | solution.py:364
  262.8 0.6 copy.10
  263.4 0.8 copy.13
  264.2 0.7 copy.14
Async XLA Ops:
  0.6 1.1 copy-start
  1.7 0.7 copy-start.1
  2.4 0.7 copy-start.2
  3.1 0.7 copy-start.3
